TPU v7x, 32 devices: a whole 2x2x4 slice. The times are simulated.
32 devices in a mesh: dp: 2 (over y), section: 4 (over x, core), mp: 4 (over z).
Axes of the slice: x: 2, y: 2, z: 4, core: 2. Of those that a mesh axis runs over, the one named last changes fastest.
Arguments:
- hidden_in: bfloat16 [4, 128, 4096], P('dp')
- slot_hidden: bfloat16 [4, 4, 16, 4096], P('section', 'dp'), may hold values from -6 to 6
- norm_gain: float32 [4, 4096], P('section'), may hold values from 0.5 to 1.5
- w_query: bfloat16 [4, 4096, 3072], P('section', None, 'mp')
- w_key: bfloat16 [4, 4096, 1024], P('section', None, 'mp')
- w_value: bfloat16 [4, 4096, 1024], P('section', None, 'mp'), may hold values from -0.09375 to 0.09375
- w_out: bfloat16 [4, 3072, 4096], P('section', 'mp'), may hold values from -0.109375 to 0.109375
- key_a: bfloat16 [4, 4096, 64], P('section'), may hold values from -0.09375 to 0.09375
- key_b: bfloat16 [4, 64, 1024], P('section', None, 'mp'), may hold values from -0.375 to 0.375
- value_a: bfloat16 [4, 4096, 64], P('section'), may hold values from -0.09375 to 0.09375
- value_b: bfloat16 [4, 64, 1024], P('section', None, 'mp'), may hold values from -0.375 to 0.375
- cotangent: bfloat16 [4, 128, 4096], P('dp'), may hold values from -6 to 6
Outputs:
- grad_a: float32 [4, 2, 4096, 64], P('section')
- grad_b: float32 [4, 2, 64, 1024], P('section', None, None, 'mp')
All inputs are finite; a program needn't handle non-finite values.
Results may differ from a plain program's by a relative error of at most 0.028.
Values may be sent and summed in bfloat16 or wider, within the bound.
A program may use at most 128 MiB of HBM per device.

v0:
```python
import math

import jax
import jax.numpy as jnp
from jax import lax
from jax.sharding import PartitionSpec as P

HD = 128
SLOTS = 16
MICRO = 2


EPS = 1e-05
NEG = -1e30
HIGH = lax.Precision.HIGHEST


def passed_along(block, axis, distance):
    devices = range(lax.axis_size(axis))
    route = [(i - distance, i) for i in devices if i - distance in devices]
    return lax.ppermute(block, axis, route)


def normalize(rows):
    wide = rows.astype(jnp.float32)
    inverse = lax.rsqrt(jnp.mean(wide * wide, axis=-1, keepdims=True) + EPS)
    return (wide * inverse, inverse)


def visible(count, slots):
    qpos = lax.broadcasted_iota(jnp.int32, (count, slots + count), 0)
    kpos = lax.broadcasted_iota(jnp.int32, (count, slots + count), 1)
    return (kpos < slots) | (kpos - slots <= qpos)


def mixdot(left, right):
    return jnp.dot(left, right, preferred_element_type=jnp.float32)


def attend(query, keys, values):
    count = query.shape[0]
    groups = keys.shape[1] // HD
    per_group = query.shape[1] // keys.shape[1]
    q_four = query.reshape(count, groups, per_group, HD)
    k_three = keys.reshape(-1, groups, HD)
    v_three = values.reshape(-1, groups, HD)
    scores = jnp.einsum(
        "igcd,jgd->gcij", q_four, k_three, preferred_element_type=jnp.float32
    ) / math.sqrt(HD)
    scores = jnp.where(visible(count, SLOTS), scores, NEG)
    top = jnp.max(scores, axis=-1, keepdims=True)
    probs = jnp.exp(scores - top)
    probs = probs / jnp.sum(probs, axis=-1, keepdims=True)
    weights = probs.astype(jnp.bfloat16)
    mixed = jnp.einsum("gcij,jgd->igcd", weights, v_three, preferred_element_type=jnp.float32)
    return (mixed.reshape(count, -1).astype(jnp.bfloat16), probs, weights)


def attend_back(grad_mixed, query, keys, values, probs, weights):
    count = query.shape[0]
    groups = keys.shape[1] // HD
    per_group = query.shape[1] // keys.shape[1]
    q_four = query.reshape(count, groups, per_group, HD)
    k_three = keys.reshape(-1, groups, HD)
    v_three = values.reshape(-1, groups, HD)
    g_four = grad_mixed.reshape(count, groups, per_group, HD)
    grad_probs = jnp.einsum("igcd,jgd->gcij", g_four, v_three, preferred_element_type=jnp.float32)
    grad_values = jnp.einsum("gcij,igcd->jgd", weights, g_four, preferred_element_type=jnp.float32)
    grad_scores = probs * (grad_probs - jnp.sum(probs * grad_probs, axis=-1, keepdims=True))
    scaled = (grad_scores / math.sqrt(HD)).astype(jnp.bfloat16)
    grad_query = jnp.einsum("gcij,jgd->igcd", scaled, k_three, preferred_element_type=jnp.float32)
    grad_keys = jnp.einsum("gcij,igcd->jgd", scaled, q_four, preferred_element_type=jnp.float32)
    return (
        grad_query.reshape(count, -1).astype(jnp.bfloat16),
        grad_keys.reshape(-1, groups * HD),
        grad_values.reshape(-1, groups * HD),
    )


def slot_entries(slot_rows, gain, w_key, w_value, key_a, key_b, value_a, value_b):
    unit, inverse = normalize(slot_rows)
    slot_normed = (unit * gain).astype(jnp.bfloat16)
    low_key = mixdot(slot_normed, key_a).astype(jnp.bfloat16)
    low_value = mixdot(slot_normed, value_a).astype(jnp.bfloat16)
    slot_keys = (mixdot(slot_normed, w_key) + mixdot(low_key, key_b)).astype(jnp.bfloat16)
    slot_values = (mixdot(slot_normed, w_value) + mixdot(low_value, value_b)).astype(jnp.bfloat16)
    return (slot_normed, low_key, low_value, slot_keys, slot_values)


def local(
    hidden_in,
    slot_hidden,
    norm_gain,
    w_query,
    w_key,
    w_value,
    w_out,
    key_a,
    key_b,
    value_a,
    value_b,
    cotangent,
):
    gain = norm_gain[0]
    w_q = w_query[0]
    w_k = w_key[0]
    w_v = w_value[0]
    w_o = w_out[0]
    down_key = key_a[0]
    up_key = key_b[0]
    down_value = value_a[0]
    up_value = value_b[0]
    slot_all = slot_hidden[0]
    section = lax.axis_index("section")
    sections = lax.axis_size("section")
    ticks = MICRO + sections - 1
    first = section == 0
    final = section == sections - 1
    block_rows = hidden_in.shape[1]
    share = block_rows // lax.axis_size("mp")
    offset = lax.axis_index("mp") * share

    def project_all(normed):
        return (
            mixdot(normed, w_q).astype(jnp.bfloat16),
            mixdot(normed, w_k).astype(jnp.bfloat16),
            mixdot(normed, w_v).astype(jnp.bfloat16),
        )

    def attention_core(normed, slot_rows):
        query, key_tok, value_tok = project_all(normed)
        slot_normed, low_key, low_value, slot_keys, slot_values = slot_entries(
            slot_rows, gain, w_k, w_v, down_key, up_key, down_value, up_value
        )
        keys = jnp.concatenate([slot_keys, key_tok], axis=0)
        values = jnp.concatenate([slot_values, value_tok], axis=0)
        mixed, probs, weights = attend(query, keys, values)
        return (query, keys, values, mixed, probs, weights, slot_normed, low_key, low_value)

    arrive = jnp.zeros_like(hidden_in[0])
    kept_rows = jnp.zeros_like(hidden_in)
    for tick in range(ticks):
        micro = tick - section
        valid = (micro >= 0) & (micro < MICRO)
        place = jnp.clip(micro, 0, MICRO - 1)
        rows = jnp.where(first, hidden_in[min(tick, MICRO - 1)], arrive)
        kept_rows = jnp.where(
            valid, lax.dynamic_update_index_in_dim(kept_rows, rows, place, 0), kept_rows
        )
        unit, inverse = normalize(rows)
        normed = (unit * gain).astype(jnp.bfloat16)
        slot_rows = lax.dynamic_index_in_dim(slot_all, place, 0, keepdims=False)
        mixed = attention_core(normed, slot_rows)[3]
        summed = lax.psum_scatter(mixdot(mixed, w_o), "mp", scatter_dimension=0, tiled=True)
        own_rows = lax.dynamic_slice_in_dim(rows, offset, share, 0)
        own_result = (own_rows.astype(jnp.float32) + summed).astype(jnp.bfloat16)
        result = lax.all_gather(own_result, "mp", axis=0, tiled=True)
        if tick + 1 < ticks:
            arrive = passed_along(result, "section", 1)
    grad_in = jnp.zeros((share, hidden_in.shape[2]), jnp.float32)
    sum_b = jnp.zeros((2,) + up_key.shape, jnp.float32)
    low_store = jnp.zeros((2, MICRO, SLOTS, up_key.shape[0]), jnp.float32)
    slot_store = jnp.zeros((MICRO, SLOTS, hidden_in.shape[2]), jnp.bfloat16)
    for tick in range(ticks):
        micro = tick - (sections - 1 - section)
        valid = (micro >= 0) & (micro < MICRO)
        place = jnp.clip(micro, 0, MICRO - 1)
        own_cot = lax.dynamic_slice_in_dim(cotangent[min(tick, MICRO - 1)], offset, share, 0)
        grad = jnp.where(final, own_cot.astype(jnp.float32), grad_in)
        rows = lax.dynamic_index_in_dim(kept_rows, place, 0, keepdims=False)
        unit, inverse = normalize(rows)
        normed = (unit * gain).astype(jnp.bfloat16)
        slot_rows = lax.dynamic_index_in_dim(slot_all, place, 0, keepdims=False)
        query, keys, values, mixed, probs, weights, slot_normed, low_key, low_value = (
            attention_core(normed, slot_rows)
        )
        grad_low = grad.astype(jnp.bfloat16)
        grad_mixed = mixdot(lax.all_gather(grad_low, "mp", axis=0, tiled=True), w_o.T).astype(
            jnp.bfloat16
        )
        grad_query, grad_keys, grad_values = attend_back(
            grad_mixed, query, keys, values, probs, weights
        )
        key_grad = grad_keys.astype(jnp.bfloat16)
        value_grad = grad_values.astype(jnp.bfloat16)
        total = mixdot(grad_query, w_q.T)
        total = total + mixdot(
            lax.dynamic_slice_in_dim(key_grad, SLOTS, lax.axis_size("mp") * share, 0), w_k.T
        )
        grad_normed = lax.psum_scatter(
            (
                total
                + mixdot(
                    lax.dynamic_slice_in_dim(value_grad, SLOTS, lax.axis_size("mp") * share, 0),
                    w_v.T,
                )
            ).astype(jnp.bfloat16),
            "mp",
            scatter_dimension=0,
            tiled=True,
        ).astype(jnp.float32)
        own_unit = lax.dynamic_slice_in_dim(unit, offset, share, 0)
        own_inverse = lax.dynamic_slice_in_dim(inverse, offset, share, 0)
        scaled = grad_normed * gain
        grad_rows = grad + own_inverse * (
            scaled - own_unit * jnp.mean(scaled * own_unit, axis=-1, keepdims=True)
        )
        slot_key_grad = key_grad[:SLOTS]
        slot_value_grad = value_grad[:SLOTS]
        term_b = jnp.stack([mixdot(low_key.T, slot_key_grad), mixdot(low_value.T, slot_value_grad)])
        sum_b = sum_b + jnp.where(valid, term_b, 0.0)
        low_grads = jnp.stack(
            [mixdot(slot_key_grad, up_key.T), mixdot(slot_value_grad, up_value.T)]
        )
        low_store = jnp.where(
            valid, lax.dynamic_update_index_in_dim(low_store, low_grads, place, 1), low_store
        )
        slot_store = jnp.where(
            valid, lax.dynamic_update_index_in_dim(slot_store, slot_normed, place, 0), slot_store
        )
        if tick + 1 < ticks:
            grad_in = passed_along(grad_rows.astype(jnp.bfloat16), "section", -1).astype(
                grad_rows.dtype
            )
    low_total = lax.psum(low_store, "mp")
    term = jnp.einsum("msd,tmsr->tdr", slot_store.astype(jnp.float32), low_total, precision=HIGH)
    grad_a, grad_b = (
        lax.psum(term.astype(jnp.bfloat16), "dp").astype(jnp.float32),
        lax.psum(sum_b.astype(jnp.bfloat16), "dp").astype(jnp.float32),
    )
    return (grad_a[None], grad_b[None])


def solution(mesh):
    placed = (
        P("dp", None, None),
        P("section", "dp", None, None),
        P("section", None),
        P("section", None, "mp"),
        P("section", None, "mp"),
        P("section", None, "mp"),
        P("section", "mp", None),
        P("section", None, None),
        P("section", None, "mp"),
        P("section", None, None),
        P("section", None, "mp"),
        P("dp", None, None),
    )
    return jax.shard_map(
        local,
        mesh=mesh,
        in_specs=placed,
        out_specs=(P("section", None, None, None), P("section", None, None, "mp")),
        check_vma=False,
    )
```

profile of v0, /device:TPU:0, one launch (start us, length us, event | category | flops | bytes accessed | tf_op | source)
XLA Modules:
  0.0 966.5 jit_solution(5284312413350592072)
XLA Ops:
  10.0 3.9 fusion.224
  20.8 3.0 fusion.277
  30.7 5.2 fusion.30
  36.0 46.7 %reduce-scatter.9.cloned.1.call-done = f32[32,4096]{1,0:T(8,128)} async-done(((f32[128,4096]{1,0:T(8,128)}), f32[32,4096]{1,0:T(8,128)}) %reduce-scatter.9.cloned.1.call-update) | async-done | bytes 524304 | tf_op jit(solution)/shard_map/reduce_scatter | solution.py:154
  84.6 27.6 %all-gather.10.cloned.1.call-done = bf16[128,4096]{1,0:T(8,128)(2,1)} async-done(((bf16[32,4096]{1,0:T(8,128)(2,1)}), bf16[128,4096]{1,0:T(8,128)(2,1)}) %all-gather.10.cloned.1.call-update) | async-done | bytes 1048592 | tf_op jit(solution)/shard_map/all_gather | solution.py:157
  112.2 2.6 collective-permute-start
  118.4 4.9 fusion.227
  138.8 5.2 fusion.28
  144.1 55.4 %reduce-scatter.11.cloned.1.call-done = f32[32,4096]{1,0:T(8,128)} async-done(((f32[128,4096]{1,0:T(8,128)}), f32[32,4096]{1,0:T(8,128)}) %reduce-scatter.11.cloned.1.call-update) | async-done | bytes 524304 | tf_op jit(solution)/shard_map/reduce_scatter | solution.py:154
  201.4 27.4 %all-gather.12.cloned.1.call-done = bf16[128,4096]{1,0:T(8,128)(2,1)} async-done(((bf16[32,4096]{1,0:T(8,128)(2,1)}), bf16[128,4096]{1,0:T(8,128)(2,1)}) %all-gather.12.cloned.1.call-update) | async-done | bytes 1048592 | tf_op jit(solution)/shard_map/all_gather | solution.py:157
  228.8 2.8 collective-permute-start.1
  235.2 4.9 fusion.230
  255.6 5.2 fusion.26
  260.9 55.2 %reduce-scatter.13.cloned.1.call-done = f32[32,4096]{1,0:T(8,128)} async-done(((f32[128,4096]{1,0:T(8,128)}), f32[32,4096]{1,0:T(8,128)}) %reduce-scatter.13.cloned.1.call-update) | async-done | bytes 524304 | tf_op jit(solution)/shard_map/reduce_scatter | solution.py:154
  318.0 27.4 %all-gather.14.cloned.1.call-done = bf16[128,4096]{1,0:T(8,128)(2,1)} async-done(((bf16[32,4096]{1,0:T(8,128)(2,1)}), bf16[128,4096]{1,0:T(8,128)(2,1)}) %all-gather.14.cloned.1.call-update) | async-done | bytes 1048592 | tf_op jit(solution)/shard_map/all_gather | solution.py:157
  345.4 2.6 collective-permute-start.2
  351.7 4.9 fusion.233
  372.0 5.3 fusion.24
  377.4 2.8 fusion.874
  398.8 34.1 %reduce-scatter.15.cloned.1.call-done = f32[32,4096]{1,0:T(8,128)} async-done(((f32[128,4096]{1,0:T(8,128)}), f32[32,4096]{1,0:T(8,128)}) %reduce-scatter.15.cloned.1.call-update) | async-done | bytes 524304 | tf_op jit(solution)/shard_map/reduce_scatter | solution.py:154
  435.6 25.9 %all-gather.18.cloned.1.call-done = bf16[128,4096]{1,0:T(8,128)(2,1)} async-done(((bf16[32,4096]{1,0:T(8,128)(2,1)}), bf16[128,4096]{1,0:T(8,128)(2,1)}) %all-gather.18.cloned.1.call-update) | async-done | bytes 1048592 | tf_op jit(solution)/shard_map/all_gather | solution.py:178
  461.5 6.0 fusion.251
  469.3 2.5 fusion.466
  471.8 18.8 %all-gather.16.cloned.1.call-done = bf16[128,4096]{1,0:T(8,128)(2,1)} async-done(((bf16[32,4096]{1,0:T(8,128)(2,1)}), bf16[128,4096]{1,0:T(8,128)(2,1)}) %all-gather.16.cloned.1.call-update) | async-done | bytes 1048592 | tf_op jit(solution)/shard_map/all_gather | solution.py:157
  492.3 2.9 fusion.465
  495.2 2.6 fusion.464
  497.8 2.8 fusion.463
  500.6 4.2 multiply_reduce_fusion
  516.0 6.3 fusion.44
  522.6 2.6 convolution_add_fusion.7
  527.1 2.6 fusion.431
  532.8 6.4 convert_bitcast_fusion
  539.2 23.1 %reduce-scatter.17.cloned.1.call-done = bf16[32,4096]{1,0:T(8,128)(2,1)} async-done(((bf16[128,4096]{1,0:T(8,128)(2,1)}), bf16[32,4096]{1,0:T(8,128)(2,1)}) %reduce-scatter.17.cloned.1.call-update) | async-done | bytes 262160 | tf_op jit(solution)/shard_map/reduce_scatter | solution.py:190
  571.6 4.8 fusion.239
  586.8 2.6 fusion.890
  589.4 10.5 %all-gather.20.cloned.1.call-done = bf16[128,4096]{1,0:T(8,128)(2,1)} async-done(((bf16[32,4096]{1,0:T(8,128)(2,1)}), bf16[128,4096]{1,0:T(8,128)(2,1)}) %all-gather.20.cloned.1.call-update) | async-done | bytes 1048592 | tf_op jit(solution)/shard_map/all_gather | solution.py:178
  599.8 6.0 fusion.254
  614.1 2.4 convolution_convert_fusion.2
  616.5 6.5 fusion.40
  628.2 2.6 convolution_add_fusion.5
  639.2 20.2 %reduce-scatter.19.cloned.1.call-done = bf16[32,4096]{1,0:T(8,128)(2,1)} async-done(((bf16[128,4096]{1,0:T(8,128)(2,1)}), bf16[32,4096]{1,0:T(8,128)(2,1)}) %reduce-scatter.19.cloned.1.call-update) | async-done | bytes 262160 | tf_op jit(solution)/shard_map/reduce_scatter | solution.py:190
  667.6 4.8 fusion.242
  684.8 12.2 %all-gather.22.cloned.1.call-done = bf16[128,4096]{1,0:T(8,128)(2,1)} async-done(((bf16[32,4096]{1,0:T(8,128)(2,1)}), bf16[128,4096]{1,0:T(8,128)(2,1)}) %all-gather.22.cloned.1.call-update) | async-done | bytes 1048592 | tf_op jit(solution)/shard_map/all_gather | solution.py:178
  696.9 6.0 fusion.257
  713.6 6.4 fusion.36
  725.2 2.6 convolution_add_fusion.3
  735.6 20.8 %reduce-scatter.21.cloned.1.call-done = bf16[32,4096]{1,0:T(8,128)(2,1)} async-done(((bf16[128,4096]{1,0:T(8,128)(2,1)}), bf16[32,4096]{1,0:T(8,128)(2,1)}) %reduce-scatter.21.cloned.1.call-update) | async-done | bytes 262160 | tf_op jit(solution)/shard_map/reduce_scatter | solution.py:190
  764.7 4.2 fusion.245
  771.5 2.5 fusion.298
  776.7 17.2 %all-gather.24.cloned.1.call-done = bf16[128,4096]{1,0:T(8,128)(2,1)} async-done(((bf16[32,4096]{1,0:T(8,128)(2,1)}), bf16[128,4096]{1,0:T(8,128)(2,1)}) %all-gather.24.cloned.1.call-update) | async-done | bytes 1048592 | tf_op jit(solution)/shard_map/all_gather | solution.py:178
  793.9 6.0 fusion.260
  807.3 2.5 convolution_convert_fusion
  809.8 6.4 fusion.32
  816.5 2.6 convolution_add_fusion.1
  822.5 4.2 fusion.248
  831.4 2.5 fusion.301
  837.3 2.6 fusion.899
  839.9 7.7 reduce-scatter.23.cloned.1.call-done
  866.9 18.2 %all-gather.26.cloned.1.call-done = bf16[128,4096]{1,0:T(8,128)(2,1)} async-done(((bf16[32,4096]{1,0:T(8,128)(2,1)}), bf16[128,4096]{1,0:T(8,128)(2,1)}) %all-gather.26.cloned.1.call-update) | async-done | bytes 1048592 | tf_op jit(solution)/shard_map/all_gather | solution.py:178
  885.2 5.3 fusion.263
  894.5 17.6 %psum.21 = f32[2,2,16,64]{3,2,0,1:T(8,128)S(1)} all-reduce(f32[2,2,16,64]{3,2,0,1:T(8,128)S(1)} %fusion.687), channel_id=1, replica_groups=mesh['dp'=2,'section'=4,'mp'=4] {'mp'}, use_global_device_ids=true, to_apply=%region_53.54 | all-reduce | flops 4096 | bytes 32768 | tf_op jit(solution)/shard_map/psum | solution.py:225
  912.1 2.9 fusion.63
  915.8 40.0 %all-reduce.3.cloned.1.call-done = (bf16[1,2,4096,64]{2,3,1,0:T(8,128)(2,1)}, bf16[1,2,64,256]{3,2,1,0:T(8,128)(2,1)}) async-done(((bf16[1,2,4096,64]{2,3,1,0:T(8,128)(2,1)}, bf16[1,2,64,256]{3,2,1,0:T(8,128)(2,1)}), (bf16[1,2,4096,64]{2,3,1,0:T(8,128)(2,1)}, bf16[1,2,64,256]{3,2,1,0:T(8,128)(2,1)})) %all-reduce.3.cloned.1.call-update) | async-done | bytes 1114128 | tf_op jit(solution)/shard_map/psum | solution.py:228
  955.7 2.8 broadcast_in_dim.170
  (506 shorter events, 262.5 us)
Async XLA Ops:
  7.2 6.9 copy-start
  7.2 75.5 %reduce-scatter.9.cloned.1.call-start = ((), (), s32[]{:S(2)}) async-start(), calls=%async_computation.8 | async-start | bytes 2621440 | tf_op jit(solution)/shard_map/reduce_scatter | solution.py:154
  18.7 5.1 copy-start.15
  18.7 5.1 copy-start.22
  35.9 76.2 %all-gather.10.cloned.1.call-start = ((), (), s32[]{:S(2)}) async-start(), calls=%async_computation.9 | async-start | bytes 1310720 | tf_op jit(solution)/shard_map/all_gather | solution.py:157
  84.5 114.9 %reduce-scatter.11.cloned.1.call-start = ((), (), s32[]{:S(2)}) async-start(), calls=%async_computation.10 | async-start | bytes 2621440 | tf_op jit(solution)/shard_map/reduce_scatter | solution.py:154
  112.2 5.5 collective-permute-start
  118.4 6.1 copy-start.24
  144.0 87.6 %copy-start.95 = (f32[16]{0:T(128)S(1)}, f32[16]{0:T(128)}, u32[]{:S(2)}) copy-start(f32[16]{0:T(128)} %get-tuple-element.11) | copy-start | bytes 196
  144.0 84.7 %all-gather.12.cloned.1.call-start = ((), (), s32[]{:S(2)}) async-start(), calls=%async_computation.11 | async-start | bytes 1310720 | tf_op jit(solution)/shard_map/all_gather | solution.py:157
  201.3 114.7 %reduce-scatter.13.cloned.1.call-start = ((), (), s32[]{:S(2)}) async-start(), calls=%async_computation.12 | async-start | bytes 2621440 | tf_op jit(solution)/shard_map/reduce_scatter | solution.py:154
  228.8 5.7 collective-permute-start.1
  235.2 6.1 copy-start.26
  260.8 87.2 %copy-start.93 = (f32[16]{0:T(128)S(1)}, f32[16]{0:T(128)}, u32[]{:S(2)}) copy-start(f32[16]{0:T(128)} %get-tuple-element.10) | copy-start | bytes 196
  260.9 84.6 %all-gather.14.cloned.1.call-start = ((), (), s32[]{:S(2)}) async-start(), calls=%async_computation.13 | async-start | bytes 1310720 | tf_op jit(solution)/shard_map/all_gather | solution.py:157
  317.9 114.9 %reduce-scatter.15.cloned.1.call-start = ((), (), s32[]{:S(2)}) async-start(), calls=%async_computation.14 | async-start | bytes 2621440 | tf_op jit(solution)/shard_map/reduce_scatter | solution.py:154
  345.4 5.5 collective-permute-start.2
  351.6 6.1 copy-start.27
  377.3 84.2 %all-gather.18.cloned.1.call-start = ((), (), s32[]{:S(2)}) async-start(), calls=%async_computation.16 | async-start | bytes 1310720 | tf_op jit(solution)/shard_map/all_gather | solution.py:178
  377.4 5.1 copy-start.92
  382.0 108.6 %all-gather.16.cloned.1.call-start = ((), (), s32[]{:S(2)}) async-start(), calls=%async_computation.15 | async-start | bytes 1310720 | tf_op jit(solution)/shard_map/all_gather | solution.py:157
  384.6 7.9 copy-start.60
  385.0 8.8 copy-start.61
  385.3 9.2 copy-start.58
  385.6 9.6 copy-start.59
  392.7 4.9 copy-start.30
  434.7 127.6 %reduce-scatter.17.cloned.1.call-start = ((), (), s32[]{:S(2)}) async-start(), calls=%async_computation.17 | async-start | bytes 1310720 | tf_op jit(solution)/shard_map/reduce_scatter | solution.py:190
  435.6 33.7 %copy-start.25 = (bf16[128,4096]{1,0:T(8,128)(2,1)S(1)}, bf16[128,4096]{1,0:T(8,128)(2,1)}, u32[]{:S(2)}) copy-start(bf16[128,4096]{1,0:T(8,128)(2,1)} %copy-done.24) | copy-start | bytes 3145732
  471.8 23.4 %copy-start.28 = (bf16[128,4096]{1,0:T(8,128)(2,1)S(1)}, bf16[128,4096]{1,0:T(8,128)(2,1)}, u32[]{:S(2)}) copy-start(bf16[128,4096]{1,0:T(8,128)(2,1)} %copy-done.27) | copy-start | bytes 3145732
  490.6 7.2 collective-permute-start.3
  492.2 5.5 copy-start.20
  495.2 9.7 slice-start
  497.8 7.1 slice-start.1
  512.7 9.7 %copy-start.46 = (bf16[144,2,128]{2,0,1:T(8,128)(2,1)}, bf16[144,2,128]{2,0,1:T(8,128)(2,1)S(1)}, u32[]{:S(2)}) copy-start(bf16[144,2,128]{2,0,1:T(8,128)(2,1)S(1)} %fusion.339) | copy-start | bytes 221188
  514.4 7.9 copy-start.45
  527.0 5.2 copy-start.99
  527.0 72.8 %all-gather.20.cloned.1.call-start = ((), (), s32[]{:S(2)}) async-start(), calls=%async_computation.18 | async-start | bytes 1310720 | tf_op jit(solution)/shard_map/all_gather | solution.py:178
  562.4 7.0 copy-start.21
  565.2 3.4 collective-permute-start.4
  570.2 89.3 %reduce-scatter.19.cloned.1.call-start = ((), (), s32[]{:S(2)}) async-start(), calls=%async_computation.19 | async-start | bytes 1310720 | tf_op jit(solution)/shard_map/reduce_scatter | solution.py:190
  616.5 6.5 copy-start.47
  632.7 64.3 %all-gather.22.cloned.1.call-start = ((), (), s32[]{:S(2)}) async-start(), calls=%async_computation.20 | async-start | bytes 1310720 | tf_op jit(solution)/shard_map/all_gather | solution.py:178
  635.1 28.6 %copy-start.78 = (f32[16]{0:T(128)S(1)}, f32[16]{0:T(128)}, u32[]{:S(2)}) copy-start(f32[16]{0:T(128)} %copy-done.77) | copy-start | bytes 196
  661.0 6.6 copy-start.94
  662.4 3.4 collective-permute-start.5
  667.3 89.1 %reduce-scatter.21.cloned.1.call-start = ((), (), s32[]{:S(2)}) async-start(), calls=%async_computation.21 | async-start | bytes 1310720 | tf_op jit(solution)/shard_map/reduce_scatter | solution.py:190
  667.6 10.6 %copy-start.96 = (f32[128]{0:T(128)}, f32[128]{0:T(128)S(1)}, u32[]{:S(2)}) copy-start(f32[128]{0:T(128)S(1)} %add_rsqrt_fusion.5) | copy-start | bytes 1540
  713.6 6.5 copy-start.48
  729.7 64.2 %all-gather.24.cloned.1.call-start = ((), (), s32[]{:S(2)}) async-start(), calls=%async_computation.22 | async-start | bytes 1310720 | tf_op jit(solution)/shard_map/all_gather | solution.py:178
  731.5 29.2 %copy-start.76 = (f32[16]{0:T(128)S(1)}, f32[16]{0:T(128)}, u32[]{:S(2)}) copy-start(f32[16]{0:T(128)} %copy-done.75) | copy-start | bytes 196
  758.0 6.6 copy-start.91
  759.4 3.4 collective-permute-start.6
  764.3 83.4 %reduce-scatter.23.cloned.1.call-start = ((), (), s32[]{:S(2)}) async-start(), calls=%async_computation.23 | async-start | bytes 1310720 | tf_op jit(solution)/shard_map/reduce_scatter | solution.py:190
  771.5 5.2 copy-start.50
  809.8 6.4 copy-start.49
  809.8 6.6 slice-start.2
  820.9 64.3 %all-gather.26.cloned.1.call-start = ((), (), s32[]{:S(2)}) async-start(), calls=%async_computation.24 | async-start | bytes 1310720 | tf_op jit(solution)/shard_map/all_gather | solution.py:178
  831.4 17.7 %copy-start.33 = (bf16[32,4096]{1,0:T(8,128)(2,1)S(1)}, bf16[32,4096]{1,0:T(8,128)(2,1)}, u32[]{:S(2)}) copy-start(bf16[32,4096]{1,0:T(8,128)(2,1)} %copy-done.32) | copy-start | bytes 786436
  851.1 5.2 collective-permute-start.7
  857.1 98.6 %all-reduce.3.cloned.1.call-start = ((), (), s32[]{:S(2)}) async-start(), calls=%async_computation.25 | async-start | bytes 2228224 | tf_op jit(solution)/shard_map/psum | solution.py:228
  866.9 23.8 %copy-start.44 = (bf16[128,768]{0,1:T(8,128)(2,1)S(1)}, bf16[128,768]{0,1:T(8,128)(2,1)}, u32[]{:S(2)}) copy-start(bf16[128,768]{0,1:T(8,128)(2,1)} %copy.128) | copy-start | bytes 589828
  866.9 23.8 %copy-start.100 = (f32[2,3,128]{2,1,0:T(4,128)S(1)}, f32[2,3,128]{2,1,0:T(4,128)}, u32[]{:S(2)}) copy-start(f32[2,3,128]{2,1,0:T(4,128)} %get-tuple-element.39) | copy-start | bytes 9220
  892.6 22.4 %copy-start.40 = (f32[1,64,256]{2,1,0:T(8,128)S(1)}, f32[1,64,256]{2,1,0:T(8,128)}, u32[]{:S(2)}) copy-start(f32[1,64,256]{2,1,0:T(8,128)} %convolution_bitcast_fusion.23) | copy-start | bytes 196612
  892.6 22.4 %copy-start.41 = (f32[1,64,256]{2,1,0:T(8,128)S(1)}, f32[1,64,256]{2,1,0:T(8,128)}, u32[]{:S(2)}) copy-start(f32[1,64,256]{2,1,0:T(8,128)} %convolution_bitcast_fusion.24) | copy-start | bytes 196612
  (66 other events, 174.0 us)
Sparse Core Ops, SparseCore 0:
  36.1 46.5 reduce-scatter.8
  84.9 27.2 all-gather.9
  144.2 55.2 reduce-scatter.10
  201.5 27.2 all-gather.11
  261.0 55.0 reduce-scatter.12
  318.1 27.2 all-gather.13
  377.5 55.3 reduce-scatter.14
  434.4 27.0 all-gather.17
  463.1 27.4 all-gather.15
  527.1 35.1 reduce-scatter.16
  570.3 29.4 all-gather.19
  632.8 26.6 reduce-scatter.18
  667.5 29.4 all-gather.21
  729.8 26.6 reduce-scatter.20
  764.4 29.4 all-gather.23
  821.0 26.6 reduce-scatter.22
  857.3 27.8 all-gather.25
  915.9 39.8 all-reduce.2
where the time goes:
time: 979 us; the launch traced here: 967 us
  waiting for transfers between devices  492 us (50%)
  matrix products  282 us (29%)
  other arithmetic  76.7 us (8%)
  local copies, waits for them, and re-layouts  64.7 us (7%)
  blocking collectives  17.6 us (2%)
  starting transfers between devices  17 us (2%)
  between operations  16.4 us (2%)
    dot_general x114, matrix products, mixdot(): return jnp.dot(left, right, preferred_element_type=jnp.float32)  215 us
    reduce_scatter x4, waiting for transfers between devices, local(): lax.psum_scatter(mixdot(mixed, w_o), 'mp', scatter_dimension=0, tiled=True)  191 us
    all_gather x4, waiting for transfers between devices, local(): result = lax.all_gather(own_result, 'mp', axis=0, tiled=True)  101 us
    all_gather x5, waiting for transfers between devices, local(): lax.all_gather(grad_low, 'mp', axis=0, tiled=True)  84 us
    reduce_scatter x4, waiting for transfers between devices, local(): lax.psum_scatter((total + mixdot(lax.dynamic_slice_in_dim(value_grad, SLO...  71.9 us
    psum x1, waiting for transfers between devices, local(): lax.psum(term.astype(jnp.bfloat16), 'dp').astype(jnp.float32)  40 us
  transfers between devices with their start and end apart: 26, of which 21 were waited for; matrix products, arithmetic and copies ran while one was open for 16% of the time, Pallas kernels for 0%

commit v1 on v0

v1 whole, which is shorter than its diff:
```python
import functools
import math

import jax
import jax.numpy as jnp
from jax import lax
from jax.experimental import pallas as pl
from jax.experimental.pallas import tpu as pltpu
from jax.sharding import PartitionSpec as P

HD = 128
EPS = 1e-05
NEG = -1e30
HIGH = lax.Precision.HIGHEST
MESH = pl.DeviceIdType.MESH
CHUNKS = 4
F32 = jnp.float32
BF16 = jnp.bfloat16


def dot(a, b):
    return jnp.dot(a, b, preferred_element_type=F32)


def dot_nt(a, b):
    return lax.dot_general(a, b, (((1,), (1,)), ((), ())), preferred_element_type=F32)


def dot_tn(a, b):
    return lax.dot_general(a, b, (((0,), (0,)), ((), ())), preferred_element_type=F32)


def kernel(
    ndp,
    nsec,
    nmp,
    hidden,
    slots,
    gain,
    w_q,
    w_k,
    w_v,
    w_out,
    key_a,
    key_b,
    value_a,
    value_b,
    cot,
    sn_out,
    low_out,
    low_total_out,
    ks_out,
    w_all,
    w_o,
    rows,
    grads,
    xn,
    part_f,
    part_b,
    rs_f,
    rs_b,
    own_f,
    own_b,
    q,
    kpad,
    vpad,
    probs,
    mixed,
    gmix,
    dqkv,
    sn_all,
    low_all,
    lg_all,
    ks_all,
    w_sem,
    in_sem,
    rsf_s,
    rsf_r,
    rsb_s,
    rsb_r,
    agf_s,
    agf_r,
    agb_s,
    agb_r,
    sn_s,
    sn_r,
    lo_s,
    lo_r,
    lg_s,
    lg_r,
    ks_s,
    ks_r,
):
    dp = lax.axis_index("dp")
    sec = lax.axis_index("section")
    mp = lax.axis_index("mp")
    last = nsec - 1
    nb, count, width = rows.shape
    ns = slots.shape[1] // nb
    share = count // nmp
    ch = width // CHUNKS
    qw = q.shape[2]
    kw = kpad.shape[2]
    groups = kw // HD
    per = qw // kw
    padded = kpad.shape[1]
    scale = 1.0 / math.sqrt(HD)

    loads = [
        pltpu.make_async_copy(w_k.at[0], w_all.at[:, pl.ds(qw, kw)], w_sem.at[0]),
        pltpu.make_async_copy(w_v.at[0], w_all.at[:, pl.ds(qw + kw, kw)], w_sem.at[1]),
        pltpu.make_async_copy(w_q.at[0], w_all.at[:, pl.ds(0, qw)], w_sem.at[2]),
        pltpu.make_async_copy(w_out.at[0], w_o, w_sem.at[3]),
    ]
    for load in loads:
        load.start()
    load_rows = pltpu.make_async_copy(hidden, rows, in_sem.at[0])
    load_cot = pltpu.make_async_copy(cot, grads, in_sem.at[1])

    @pl.when(sec == 0)
    def _():
        load_rows.start()

    @pl.when(sec == last)
    def _():
        load_cot.start()

    bar = pltpu.get_barrier_semaphore()
    for a in range(ndp):
        for b in range(nmp):
            if a or b:
                pl.semaphore_signal(
                    bar,
                    inc=1,
                    device_id={"dp": lax.rem(dp + a, ndp), "mp": lax.rem(mp + b, nmp)},
                    device_id_type=MESH,
                )

    @pl.when(sec < last)
    def _():
        for b in range(nmp):
            pl.semaphore_signal(
                bar, inc=1, device_id={"section": sec + 1, "mp": b}, device_id_type=MESH
            )

    @pl.when(sec > 0)
    def _():
        for b in range(nmp):
            pl.semaphore_signal(
                bar, inc=1, device_id={"section": sec - 1, "mp": b}, device_id_type=MESH
            )

    edge = jnp.where((sec == 0) | (sec == last), nmp, 2 * nmp)
    pl.semaphore_wait(bar, ndp * nmp - 1 + edge)

    def dp_copy(buf, send, recv, a, source):
        return pltpu.make_async_remote_copy(
            src_ref=buf.at[source],
            dst_ref=buf.at[source],
            send_sem=send.at[a - 1],
            recv_sem=recv.at[a - 1],
            device_id={"dp": lax.rem(dp + a, ndp)},
            device_id_type=MESH,
        )

    def dp_send(buf, send, recv):
        for a in range(1, ndp):
            dp_copy(buf, send, recv, a, dp).start()

    def dp_wait(buf, send, recv):
        for a in range(1, ndp):
            dp_copy(buf, send, recv, a, lax.rem(dp - a + ndp, ndp)).wait_recv()
        for a in range(1, ndp):
            dp_copy(buf, send, recv, a, dp).wait_send()

    wide = slots[0].astype(F32)
    inverse = lax.rsqrt(jnp.mean(wide * wide, axis=-1, keepdims=True) + EPS)
    sn_all[dp] = (wide * inverse * gain[...]).astype(BF16)
    dp_send(sn_all, sn_s, sn_r)
    sn = sn_all[dp]
    low_k = dot(sn, key_a[0]).astype(BF16)
    low_v = dot(sn, value_a[0]).astype(BF16)
    low_all[dp, 0] = low_k
    low_all[dp, 1] = low_v
    dp_send(low_all, lo_s, lo_r)
    loads[0].wait()
    slot_k = (dot(sn, w_all[:, qw : qw + kw]) + dot(low_k, key_b[0])).astype(BF16)
    loads[1].wait()
    slot_v = (dot(sn, w_all[:, qw + kw : qw + 2 * kw]) + dot(low_v, value_b[0])).astype(BF16)
    kpad[...] = jnp.zeros_like(kpad)
    vpad[...] = jnp.zeros_like(vpad)
    for m in range(nb):
        kpad[m, count : count + ns, :] = slot_k[m * ns : (m + 1) * ns]
        vpad[m, count : count + ns, :] = slot_v[m * ns : (m + 1) * ns]
    loads[2].wait()
    loads[3].wait()

    @pl.when(sec == 0)
    def _():
        load_rows.wait()

    @pl.when(sec == last)
    def _():
        load_cot.wait()

    def cols(c):
        return pl.ds(pl.multiple_of(c * ch, ch), ch)

    def share_rows(j):
        return pl.ds(pl.multiple_of(j * share, share), share)

    def sem_at(m, c, j):
        return (m * CHUNKS + c) * nmp + j

    def rs_copy(part, land, send, recv, m, c, to, source):
        return pltpu.make_async_remote_copy(
            src_ref=part.at[m, share_rows(to), cols(c)],
            dst_ref=land.at[m, source, :, cols(c)],
            send_sem=send.at[sem_at(m, c, to)],
            recv_sem=recv.at[sem_at(m, c, source)],
            device_id={"mp": to},
            device_id_type=MESH,
        )

    def ag_copy(own, land, send, recv, m, c, to, source, section):
        return pltpu.make_async_remote_copy(
            src_ref=own.at[m, :, cols(c)],
            dst_ref=land.at[m, share_rows(source), cols(c)],
            send_sem=send.at[sem_at(m, c, to)],
            recv_sem=recv.at[sem_at(m, c, source)],
            device_id={"section": section, "mp": to},
            device_id_type=MESH,
        )

    def peer(d):
        return lax.rem(mp + d, nmp)

    def rs_send(part, land, send, recv, m, c):
        for d in range(1, nmp):
            rs_copy(part, land, send, recv, m, c, peer(d), mp).start()

    def rs_wait(part, land, send, recv, m, c):
        for d in range(1, nmp):
            rs_copy(part, land, send, recv, m, c, peer(d), peer(d)).wait_recv()

    def ag_send(own, land, send, recv, m, c, section):
        for d in range(nmp):
            ag_copy(own, land, send, recv, m, c, peer(d), mp, section).start()

    def ag_wait(own, land, send, recv, m, section):
        @pl.loop(0, CHUNKS)
        def _(c):
            for j in range(nmp):
                ag_copy(own, land, send, recv, m, c, j, j, section).wait_recv()

    def rs_total(part, land, m, c):
        total = part[m, share_rows(mp), cols(c)].astype(F32)
        for d in range(1, nmp):
            total = total + land[m, peer(d), :, cols(c)].astype(F32)
        return total

    def stacked(ref, lead, g):
        parts = []
        for h in range(per):
            low = (g * per + h) * HD
            if lead is None:
                parts.append(ref[:, low : low + HD])
            else:
                parts.append(ref[lead, :, low : low + HD])
        return jnp.concatenate(parts, axis=0)

    def forward(m):
        @pl.when(sec > 0)
        def _():
            ag_wait(own_f, rows, agf_s, agf_r, m, sec - 1)

        @pl.loop(0, count // 16)
        def _(i):
            at = pl.ds(pl.multiple_of(i * 16, 16), 16)
            x = rows[m, at, :].astype(F32)
            inv = lax.rsqrt(jnp.mean(x * x, axis=-1, keepdims=True) + EPS)
            xn[at, :] = (x * inv * gain[...]).astype(BF16)

        @pl.loop(0, per)
        def _(i):
            at = pl.ds(pl.multiple_of(i * kw, kw), kw)
            q[m, :, at] = dot(xn[...], w_all[:, at]).astype(BF16)

        kpad[m, 0:count, :] = dot(xn[...], w_all[:, qw : qw + kw]).astype(BF16)
        vpad[m, 0:count, :] = dot(xn[...], w_all[:, qw + kw : qw + 2 * kw]).astype(BF16)
        i_at = lax.rem(lax.broadcasted_iota(jnp.int32, (per * count, padded), 0), count)
        j_at = lax.broadcasted_iota(jnp.int32, (per * count, padded), 1)
        seen = (j_at <= i_at) | ((j_at >= count) & (j_at < count + ns))
        for g in range(groups):
            gc = slice(g * HD, (g + 1) * HD)
            scores = dot_nt(stacked(q, m, g), kpad[m, :, gc]) * scale
            scores = jnp.where(seen, scores, NEG)
            e = jnp.exp(scores - jnp.max(scores, axis=-1, keepdims=True))
            p = e / jnp.sum(e, axis=-1, keepdims=True)
            probs[m, g] = p
            o = dot(p.astype(BF16), vpad[m, :, gc]).astype(BF16)
            for h in range(per):
                low = (g * per + h) * HD
                mixed[:, low : low + HD] = o[h * count : (h + 1) * count]

        @pl.when(sec < last)
        def _():
            @pl.loop(0, CHUNKS)
            def _(c):
                part_f[m, :, cols(c)] = dot(mixed[...], w_o[:, cols(c)]).astype(BF16)
                rs_send(part_f, rs_f, rsf_s, rsf_r, m, c)

    def forward_reduce(m):
        @pl.loop(0, CHUNKS)
        def _(c):
            rs_wait(part_f, rs_f, rsf_s, rsf_r, m, c)
            total = rs_total(part_f, rs_f, m, c)
            total = total + rows[m, share_rows(mp), cols(c)].astype(F32)
            own_f[m, :, cols(c)] = total.astype(BF16)
            ag_send(own_f, rows, agf_s, agf_r, m, c, sec + 1)

    def backward(m):
        @pl.when(sec < last)
        def _():
            ag_wait(own_b, grads, agb_s, agb_r, m, sec + 1)

        @pl.loop(0, per)
        def _(i):
            at = pl.ds(pl.multiple_of(i * kw, kw), kw)
            gmix[:, at] = dot_nt(grads[m], w_o[at, :]).astype(BF16)

        at_slot = pl.ds(pl.multiple_of(m * ns, ns), ns)
        for g in range(groups):
            gc = slice(g * HD, (g + 1) * HD)
            gm = stacked(gmix, None, g)
            p = probs[m, g]
            kg = kpad[m, :, gc]
            gp = dot_nt(gm, vpad[m, :, gc])
            gv = dot_tn(p.astype(BF16), gm).astype(BF16)
            gs = p * (gp - jnp.sum(p * gp, axis=-1, keepdims=True))
            gs = (gs * scale).astype(BF16)
            gq = dot(gs, kg).astype(BF16)
            gk = dot_tn(gs, stacked(q, m, g)).astype(BF16)
            for h in range(per):
                low = (g * per + h) * HD
                dqkv[:, low : low + HD] = gq[h * count : (h + 1) * count]
            dqkv[:, qw + g * HD : qw + (g + 1) * HD] = gk[:count]
            dqkv[:, qw + kw + g * HD : qw + kw + (g + 1) * HD] = gv[:count]
            ks_all[dp, 0, at_slot, gc] = gk[count : count + ns]
            ks_all[dp, 1, at_slot, gc] = gv[count : count + ns]

        @pl.when(sec > 0)
        def _():
            @pl.loop(0, CHUNKS)
            def _(c):
                part_b[m, :, cols(c)] = dot_nt(dqkv[...], w_all[cols(c), :]).astype(BF16)
                rs_send(part_b, rs_b, rsb_s, rsb_r, m, c)

    def backward_reduce(m):
        @pl.loop(0, CHUNKS)
        def _(c):
            rs_wait(part_b, rs_b, rsb_s, rsb_r, m, c)

        mine = share_rows(mp)
        x = rows[m, mine, :].astype(F32)
        inv = lax.rsqrt(jnp.mean(x * x, axis=-1, keepdims=True) + EPS)
        unit = x * inv
        total = part_b[m, mine, :].astype(F32)
        for d in range(1, nmp):
            total = total + rs_b[m, peer(d)].astype(F32)
        scaled = total * gain[...]
        mean = jnp.mean(scaled * unit, axis=-1, keepdims=True)
        own_b[m] = (grads[m, mine, :].astype(F32) + inv * (scaled - unit * mean)).astype(BF16)

        @pl.loop(0, CHUNKS)
        def _(c):
            ag_send(own_b, grads, agb_s, agb_r, m, c, sec - 1)

    back_at = jnp.where(sec == last, 0, nb)

    @pl.loop(0, 2 * nb + 1)
    def _(t):
        @pl.when(t < nb)
        def _():
            forward(t)

        @pl.when((sec < last) & (t >= 1) & (t < nb + 1))
        def _():
            forward_reduce(t - 1)

        @pl.when((t >= back_at) & (t < back_at + nb))
        def _():
            backward(t - back_at)

        @pl.when((sec > 0) & (t >= back_at + 1) & (t < back_at + nb + 1))
        def _():
            backward_reduce(t - back_at - 1)

    dp_send(ks_all, ks_s, ks_r)
    me = dp * nmp + mp
    lg_all[me, 0] = dot_nt(ks_all[dp, 0], key_b[0])
    lg_all[me, 1] = dot_nt(ks_all[dp, 1], value_b[0])

    def lg_copy(a, b, source):
        return pltpu.make_async_remote_copy(
            src_ref=lg_all.at[source],
            dst_ref=lg_all.at[source],
            send_sem=lg_s.at[a * nmp + b],
            recv_sem=lg_r.at[a * nmp + b],
            device_id={"dp": lax.rem(dp + a, ndp), "mp": lax.rem(mp + b, nmp)},
            device_id_type=MESH,
        )

    others = [(a, b) for a in range(ndp) for b in range(nmp) if a or b]
    for a, b in others:
        lg_copy(a, b, me).start()
    dp_wait(sn_all, sn_s, sn_r)
    dp_wait(low_all, lo_s, lo_r)
    sn_out[...] = sn_all[...]
    low_out[...] = low_all[...]
    dp_wait(ks_all, ks_s, ks_r)
    ks_out[...] = ks_all[...]
    for a, b in others:
        source = lax.rem(dp - a + ndp, ndp) * nmp + lax.rem(mp - b + nmp, nmp)
        lg_copy(a, b, source).wait_recv()
    for a in range(ndp):
        total = lg_all[a * nmp]
        for b in range(1, nmp):
            total = total + lg_all[a * nmp + b]
        low_total_out[a] = total
    for a, b in others:
        lg_copy(a, b, me).wait_send()

    @pl.when(sec < last)
    def _():
        @pl.loop(0, nb * CHUNKS)
        def _(i):
            m, c = i // CHUNKS, lax.rem(i, CHUNKS)
            for d in range(1, nmp):
                rs_copy(part_f, rs_f, rsf_s, rsf_r, m, c, peer(d), mp).wait_send()
            for d in range(nmp):
                ag_copy(own_f, rows, agf_s, agf_r, m, c, peer(d), mp, sec + 1).wait_send()

    @pl.when(sec > 0)
    def _():
        @pl.loop(0, nb * CHUNKS)
        def _(i):
            m, c = i // CHUNKS, lax.rem(i, CHUNKS)
            for d in range(1, nmp):
                rs_copy(part_b, rs_b, rsb_s, rsb_r, m, c, peer(d), mp).wait_send()
            for d in range(nmp):
                ag_copy(own_b, grads, agb_s, agb_r, m, c, peer(d), mp, sec - 1).wait_send()


def local(ndp, nsec, nmp, hidden_in, slot_hidden, norm_gain, w_query, w_key, w_value, w_out,
          key_a, key_b, value_a, value_b, cotangent):
    nb, count, width = hidden_in.shape
    ns = slot_hidden.shape[2]
    qw, kw = w_query.shape[2], w_key.shape[2]
    rank = key_a.shape[2]
    share = count // nmp
    groups = kw // HD
    per = qw // kw
    padded = -(-(count + ns) // 256) * 256
    total_slots = nb * ns
    slots = slot_hidden.reshape(1, total_slots, width)
    vmem = pl.BlockSpec(memory_space=pltpu.VMEM)
    hbm = pl.BlockSpec(memory_space=pl.ANY)
    dma = pltpu.SemaphoreType.DMA
    many = dma((nb * CHUNKS * nmp,))
    few = dma((max(ndp - 1, 1),))
    sn_shape = (ndp, total_slots, width)
    low_shape = (ndp, 2, total_slots, rank)
    ks_shape = (ndp, 2, total_slots, kw)
    sn_all, low_all, low_total, ks_all = pl.pallas_call(
        functools.partial(kernel, ndp, nsec, nmp),
        out_shape=(
            jax.ShapeDtypeStruct(sn_shape, BF16),
            jax.ShapeDtypeStruct(low_shape, BF16),
            jax.ShapeDtypeStruct(low_shape, F32),
            jax.ShapeDtypeStruct(ks_shape, BF16),
        ),
        in_specs=[hbm, vmem, vmem, hbm, hbm, hbm, hbm, vmem, vmem, vmem, vmem, hbm],
        out_specs=(vmem, vmem, vmem, vmem),
        scratch_shapes=[
            pltpu.VMEM((width, qw + 2 * kw), BF16),
            pltpu.VMEM((qw, width), BF16),
            pltpu.VMEM((nb, count, width), BF16),
            pltpu.VMEM((nb, count, width), BF16),
            pltpu.VMEM((count, width), BF16),
            pltpu.VMEM((nb, count, width), BF16),
            pltpu.VMEM((nb, count, width), BF16),
            pltpu.VMEM((nb, nmp, share, width), BF16),
            pltpu.VMEM((nb, nmp, share, width), BF16),
            pltpu.VMEM((nb, share, width), BF16),
            pltpu.VMEM((nb, share, width), BF16),
            pltpu.VMEM((nb, count, qw), BF16),
            pltpu.VMEM((nb, padded, kw), BF16),
            pltpu.VMEM((nb, padded, kw), BF16),
            pltpu.VMEM((nb, groups, per * count, padded), F32),
            pltpu.VMEM((count, qw), BF16),
            pltpu.VMEM((count, qw), BF16),
            pltpu.VMEM((count, qw + 2 * kw), BF16),
            pltpu.VMEM(sn_shape, BF16),
            pltpu.VMEM(low_shape, BF16),
            pltpu.VMEM((ndp * nmp, 2, total_slots, rank), F32),
            pltpu.VMEM(ks_shape, BF16),
            dma((4,)),
            dma((2,)),
            many, many, many, many, many, many, many, many,
            few, few, few, few,
            dma((ndp * nmp,)), dma((ndp * nmp,)),
            few, few,
        ],
        compiler_params=pltpu.CompilerParams(
            collective_id=0, has_side_effects=True, vmem_limit_bytes=58 * 1024 * 1024
        ),
    )(hidden_in, slots, norm_gain, w_query, w_key, w_value, w_out, key_a, key_b, value_a, value_b,
      cotangent)
    grad_a = jnp.einsum("psd,ptsr->tdr", sn_all.astype(F32), low_total, precision=HIGH)
    grad_b = jnp.einsum("ptsr,ptsc->trc", low_all, ks_all, preferred_element_type=F32)
    return (grad_a[None], grad_b[None])


def solution(mesh):
    placed = (
        P("dp", None, None),
        P("section", "dp", None, None),
        P("section", None),
        P("section", None, "mp"),
        P("section", None, "mp"),
        P("section", None, "mp"),
        P("section", "mp", None),
        P("section", None, None),
        P("section", None, "mp"),
        P("section", None, None),
        P("section", None, "mp"),
        P("dp", None, None),
    )
    return jax.shard_map(
        functools.partial(local, mesh.shape["dp"], mesh.shape["section"], mesh.shape["mp"]),
        mesh=mesh,
        in_specs=placed,
        out_specs=(P("section", None, None, None), P("section", None, None, "mp")),
        check_vma=False,
    )
```

time: 979 us -> 323 us (0.33); the launches traced: 967 us -> 323 us
  waiting for transfers between devices: 492 us -> 0 us
  Pallas kernels: 0 us -> 313 us
  matrix products: 282 us -> 4.32 us
  other arithmetic: 76.7 us -> 0 us
  local copies, waits for them, and re-layouts: 64.7 us -> 4.72 us
  blocking collectives: 17.6 us -> 0 us
  starting transfers between devices: 17 us -> 0 us
  between operations: 16.4 us -> 0.66 us
    pallas_call x0 -> x1, Pallas kernels: none -> 313 us  [local(): pl.pallas_call(functools.partial(kernel, ndp, nsec, nmp), out_shape=(jax....]
    dot_general x142 -> x2, matrix products: 268 us -> 4.32 us  [the longest x1 3.46 us: local(): jnp.einsum('psd,ptsr->tdr', sn_all.astype(F32), low_total, precision=HIGH)]
    reduce_scatter x8 -> x0, waiting for transfers between devices: 263 us -> none  [the longest x4 191 us: local(): lax.psum_scatter(mixdot(mixed, w_o), 'mp', scatter_dimension=0, tiled=True)]
    all_gather x9 -> x0, waiting for transfers between devices: 185 us -> none  [the longest x4 101 us: local(): result = lax.all_gather(own_result, 'mp', axis=0, tiled=True)]
    psum x1 -> x0, waiting for transfers between devices: 40 us -> none  [local(): lax.psum(term.astype(jnp.bfloat16), 'dp').astype(jnp.float32)]
    convert_element_type x14 -> x0, other arithmetic: 24 us -> none  [the longest x4 7.41 us: local(): own_result = (own_rows.astype(jnp.float32) + summed).astype(jnp.bfloat16)]
    reshape x18 -> x0, local copies, waits for them, and re-layouts: 19.8 us -> none  [the longest x9 8.39 us: attend(): k_three = keys.reshape(-1, groups, HD)]
    select_n x15 -> x0, other arithmetic: 19.5 us -> none  [the longest x5 12 us: local(): jnp.where(valid, lax.dynamic_update_index_in_dim(kept_rows, rows, place,...]
  transfers between devices with their start and end apart: 26 -> 0, of which waited for: 21 -> 0; matrix products, arithmetic and copies ran while one was open for 16% -> 0% of each run, Pallas kernels for 0% -> 0%
where the time goes in v1:
time: 323 us
  Pallas kernels  313 us (97%)
  local copies, waits for them, and re-layouts  4.72 us (1%)
  matrix products  4.32 us (1%)
    pallas_call x1, Pallas kernels, local(): pl.pallas_call(functools.partial(kernel, ndp, nsec, nmp), out_shape=(jax....  313 us

profile of v1, /device:TPU:0, one launch (start us, length us, event | category | flops | bytes accessed | tf_op | source)
XLA Modules:
  0.0 322.5 jit_solution(12115067455010751143)
XLA Ops:
  0.6 2.4 copy.14.key_a
  3.0 2.4 copy.15.value_a
  5.3 312.8 %shard_map.131 = (bf16[2,32,4096]{2,1,0:T(8,128)(2,1)}, bf16[2,2,32,64]{3,2,1,0:T(8,128)(2,1)}, f32[2,2,32,64]{3,2,1,0:T(8,128)}, bf16[2,2,32,256]{3,2,1,0:T(8,128)(2,1)}) custom-call(bf16[2,128,4096]{2,1,0:T(8,128)(2,1)} %hidden.1, bf16[1,32,4096]{2,1,0:T(8,128)(2,1)} %bitcast.18, f32[1,4096]{1,0:T(1,128)} %gain.1, bf16[1,4096,768]{2,1,0:T(8,128)(2,1)} %w_q.1, ...), custom_call_target="tpu_custom_call" | custom-call | tf_op jit(solution)/shard_map/pallas_call | solution.py:475
  318.2 0.0 copy-start
  318.2 0.0 copy-start.1
  318.2 3.5 %convolution_bitcast_fusion = f32[1,2,4096,64]{2,3,1,0:T(8,128)} fusion(f32[2,2,32,64]{3,2,1,0:T(8,128)} %get-tuple-element.6, bf16[2,32,4096]{2,1,0:T(8,128)(2,1)} %get-tuple-element.7), kind=kOutput, calls=%fused_computation | convolution fusion | flops 402653184 | bytes 2654208 | tf_op jit(solution)/shard_map/psd,ptsr->tdr/dot_general | solution.py:520
  321.7 0.0 copy-done
  321.7 0.0 copy-done.1
  321.7 0.9 convolution_bitcast_fusion.1
Async XLA Ops:
  318.2 3.5 %copy-start = (bf16[2,2,32,256]{3,2,1,0:T(8,128)(2,1)S(1)}, bf16[2,2,32,256]{3,2,1,0:T(8,128)(2,1)}, u32[]{:S(2)}) copy-start(bf16[2,2,32,256]{3,2,1,0:T(8,128)(2,1)} %get-tuple-element.9) | copy-start | bytes 196612
  318.2 3.5 %copy-start.1 = (bf16[2,2,32,64]{3,2,1,0:T(8,128)(2,1)S(1)}, bf16[2,2,32,64]{3,2,1,0:T(8,128)(2,1)}, u32[]{:S(2)}) copy-start(bf16[2,2,32,64]{3,2,1,0:T(8,128)(2,1)} %get-tuple-element.8) | copy-start | bytes 49156

commit v2 on v1

--- a/solution.py
+++ b/solution.py
@@ -65,6 +65,7 @@
     kpad,
     vpad,
     probs,
+    inv_all,
     mixed,
     gmix,
     dqkv,
@@ -95,6 +96,8 @@
     sec = lax.axis_index("section")
     mp = lax.axis_index("mp")
     last = nsec - 1
+    half = nsec // 2
+    mate = lax.rem(sec + half, nsec)
     nb, count, width = rows.shape
     ns = slots.shape[1] // nb
     share = count // nmp
@@ -126,32 +129,24 @@
         load_cot.start()
 
     bar = pltpu.get_barrier_semaphore()
-    for a in range(ndp):
+    for a in range(nsec):
         for b in range(nmp):
             if a or b:
                 pl.semaphore_signal(
                     bar,
                     inc=1,
-                    device_id={"dp": lax.rem(dp + a, ndp), "mp": lax.rem(mp + b, nmp)},
+                    device_id={"section": lax.rem(sec + a, nsec), "mp": lax.rem(mp + b, nmp)},
                     device_id_type=MESH,
                 )
-
-    @pl.when(sec < last)
-    def _():
+    for a in range(1, ndp):
         for b in range(nmp):
             pl.semaphore_signal(
-                bar, inc=1, device_id={"section": sec + 1, "mp": b}, device_id_type=MESH
+                bar,
+                inc=1,
+                device_id={"dp": lax.rem(dp + a, ndp), "mp": lax.rem(mp + b, nmp)},
+                device_id_type=MESH,
             )
-
-    @pl.when(sec > 0)
-    def _():
-        for b in range(nmp):
-            pl.semaphore_signal(
-                bar, inc=1, device_id={"section": sec - 1, "mp": b}, device_id_type=MESH
-            )
-
-    edge = jnp.where((sec == 0) | (sec == last), nmp, 2 * nmp)
-    pl.semaphore_wait(bar, ndp * nmp - 1 + edge)
+    pl.semaphore_wait(bar, nsec * nmp - 1 + (ndp - 1) * nmp)
 
     def dp_copy(buf, send, recv, a, source):
         return pltpu.make_async_remote_copy(
@@ -178,8 +173,8 @@
     sn_all[dp] = (wide * inverse * gain[...]).astype(BF16)
     dp_send(sn_all, sn_s, sn_r)
     sn = sn_all[dp]
-    low_k = dot(sn, key_a[0]).astype(BF16)
-    low_v = dot(sn, value_a[0]).astype(BF16)
+    low_k = dot_nt(sn, key_a[0]).astype(BF16)
+    low_v = dot_nt(sn, value_a[0]).astype(BF16)
     low_all[dp, 0] = low_k
     low_all[dp, 1] = low_v
     dp_send(low_all, lo_s, lo_r)
@@ -203,6 +198,8 @@
     def _():
         load_cot.wait()
 
+    mine = lax.broadcasted_iota(jnp.int32, (count, 1), 0) // share == mp
+
     def cols(c):
         return pl.ds(pl.multiple_of(c * ch, ch), ch)
 
@@ -218,7 +215,7 @@
             dst_ref=land.at[m, source, :, cols(c)],
             send_sem=send.at[sem_at(m, c, to)],
             recv_sem=recv.at[sem_at(m, c, source)],
-            device_id={"mp": to},
+            device_id={"section": mate, "mp": to},
             device_id_type=MESH,
         )
 
@@ -236,12 +233,8 @@
         return lax.rem(mp + d, nmp)
 
     def rs_send(part, land, send, recv, m, c):
-        for d in range(1, nmp):
+        for d in range(nmp):
             rs_copy(part, land, send, recv, m, c, peer(d), mp).start()
-
-    def rs_wait(part, land, send, recv, m, c):
-        for d in range(1, nmp):
-            rs_copy(part, land, send, recv, m, c, peer(d), peer(d)).wait_recv()
 
     def ag_send(own, land, send, recv, m, c, section):
         for d in range(nmp):
@@ -253,11 +246,17 @@
             for j in range(nmp):
                 ag_copy(own, land, send, recv, m, c, j, j, section).wait_recv()
 
-    def rs_total(part, land, m, c):
-        total = part[m, share_rows(mp), cols(c)].astype(F32)
-        for d in range(1, nmp):
-            total = total + land[m, peer(d), :, cols(c)].astype(F32)
-        return total
+    def reduce(own, part, land, spread, rs_s, rs_r, ag_s, ag_r, m, section):
+        @pl.loop(0, CHUNKS)
+        def _(c):
+            total = None
+            for j in range(nmp):
+                rs_copy(part, land, rs_s, rs_r, m, c, j, j).wait_recv()
+            for j in range(nmp):
+                piece = land[m, j, :, cols(c)].astype(F32)
+                total = piece if total is None else total + piece
+            own[m, :, cols(c)] = total.astype(BF16)
+            ag_send(own, spread, ag_s, ag_r, m, c, section)
 
     def stacked(ref, lead, g):
         parts = []
@@ -272,7 +271,7 @@
     def forward(m):
         @pl.when(sec > 0)
         def _():
-            ag_wait(own_f, rows, agf_s, agf_r, m, sec - 1)
+            ag_wait(own_f, rows, agf_s, agf_r, m, mate)
 
         @pl.loop(0, count // 16)
         def _(i):
@@ -280,6 +279,7 @@
             x = rows[m, at, :].astype(F32)
             inv = lax.rsqrt(jnp.mean(x * x, axis=-1, keepdims=True) + EPS)
             xn[at, :] = (x * inv * gain[...]).astype(BF16)
+            inv_all[m, at, :] = jnp.broadcast_to(inv, (16, HD))
 
         @pl.loop(0, per)
         def _(i):
@@ -307,22 +307,15 @@
         def _():
             @pl.loop(0, CHUNKS)
             def _(c):
-                part_f[m, :, cols(c)] = dot(mixed[...], w_o[:, cols(c)]).astype(BF16)
+                term = dot(mixed[...], w_o[:, cols(c)])
+                term = term + jnp.where(mine, rows[m, :, cols(c)].astype(F32), 0.0)
+                part_f[m, :, cols(c)] = term.astype(BF16)
                 rs_send(part_f, rs_f, rsf_s, rsf_r, m, c)
-
-    def forward_reduce(m):
-        @pl.loop(0, CHUNKS)
-        def _(c):
-            rs_wait(part_f, rs_f, rsf_s, rsf_r, m, c)
-            total = rs_total(part_f, rs_f, m, c)
-            total = total + rows[m, share_rows(mp), cols(c)].astype(F32)
-            own_f[m, :, cols(c)] = total.astype(BF16)
-            ag_send(own_f, rows, agf_s, agf_r, m, c, sec + 1)
 
     def backward(m):
         @pl.when(sec < last)
         def _():
-            ag_wait(own_b, grads, agb_s, agb_r, m, sec + 1)
+            ag_wait(own_b, grads, agb_s, agb_r, m, mate)
 
         @pl.loop(0, per)
         def _(i):
@@ -351,50 +344,53 @@
 
         @pl.when(sec > 0)
         def _():
+            inv = inv_all[m, :, 0:1]
+            weight = (
+                jnp.sum(dqkv[:, :qw].astype(F32) * q[m].astype(F32), axis=-1, keepdims=True)
+                + jnp.sum(
+                    dqkv[:, qw : qw + kw].astype(F32) * kpad[m, 0:count, :].astype(F32),
+                    axis=-1,
+                    keepdims=True,
+                )
+                + jnp.sum(
+                    dqkv[:, qw + kw :].astype(F32) * vpad[m, 0:count, :].astype(F32),
+                    axis=-1,
+                    keepdims=True,
+                )
+            )
+            weight = weight * inv * (1.0 / width)
+
             @pl.loop(0, CHUNKS)
             def _(c):
-                part_b[m, :, cols(c)] = dot_nt(dqkv[...], w_all[cols(c), :]).astype(BF16)
+                term = dot_nt(dqkv[...], w_all[cols(c), :]) * gain[:, cols(c)]
+                term = inv * (term - rows[m, :, cols(c)].astype(F32) * weight)
+                term = term + jnp.where(mine, grads[m, :, cols(c)].astype(F32), 0.0)
+                part_b[m, :, cols(c)] = term.astype(BF16)
                 rs_send(part_b, rs_b, rsb_s, rsb_r, m, c)
 
-    def backward_reduce(m):
-        @pl.loop(0, CHUNKS)
-        def _(c):
-            rs_wait(part_b, rs_b, rsb_s, rsb_r, m, c)
-
-        mine = share_rows(mp)
-        x = rows[m, mine, :].astype(F32)
-        inv = lax.rsqrt(jnp.mean(x * x, axis=-1, keepdims=True) + EPS)
-        unit = x * inv
-        total = part_b[m, mine, :].astype(F32)
-        for d in range(1, nmp):
-            total = total + rs_b[m, peer(d)].astype(F32)
-        scaled = total * gain[...]
-        mean = jnp.mean(scaled * unit, axis=-1, keepdims=True)
-        own_b[m] = (grads[m, mine, :].astype(F32) + inv * (scaled - unit * mean)).astype(BF16)
-
-        @pl.loop(0, CHUNKS)
-        def _(c):
-            ag_send(own_b, grads, agb_s, agb_r, m, c, sec - 1)
-
-    back_at = jnp.where(sec == last, 0, nb)
-
-    @pl.loop(0, 2 * nb + 1)
+    low_half = sec < half
+    f_at = jnp.where(low_half, 0, nb)
+    rf_at = jnp.where(low_half, nb, 0)
+    rb_at = jnp.where(low_half, 2 * nb, 3 * nb)
+    b_at = jnp.where(low_half, 3 * nb, jnp.where(sec == last, nb, 2 * nb))
+
+    @pl.loop(0, 4 * nb)
     def _(t):
-        @pl.when(t < nb)
-        def _():
-            forward(t)
-
-        @pl.when((sec < last) & (t >= 1) & (t < nb + 1))
-        def _():
-            forward_reduce(t - 1)
-
-        @pl.when((t >= back_at) & (t < back_at + nb))
-        def _():
-            backward(t - back_at)
-
-        @pl.when((sec > 0) & (t >= back_at + 1) & (t < back_at + nb + 1))
-        def _():
-            backward_reduce(t - back_at - 1)
+        @pl.when((mate < last) & (t >= rf_at) & (t < rf_at + nb))
+        def _():
+            reduce(own_f, part_f, rs_f, rows, rsf_s, rsf_r, agf_s, agf_r, t - rf_at, mate + 1)
+
+        @pl.when((t >= f_at) & (t < f_at + nb))
+        def _():
+            forward(t - f_at)
+
+        @pl.when((t >= b_at) & (t < b_at + nb))
+        def _():
+            backward(t - b_at)
+
+        @pl.when((mate > 0) & (t >= rb_at) & (t < rb_at + nb))
+        def _():
+            reduce(own_b, part_b, rs_b, grads, rsb_s, rsb_r, agb_s, agb_r, t - rb_at, mate - 1)
 
     dp_send(ks_all, ks_s, ks_r)
     me = dp * nmp + mp
@@ -431,25 +427,18 @@
     for a, b in others:
         lg_copy(a, b, me).wait_send()
 
-    @pl.when(sec < last)
-    def _():
-        @pl.loop(0, nb * CHUNKS)
-        def _(i):
-            m, c = i // CHUNKS, lax.rem(i, CHUNKS)
-            for d in range(1, nmp):
-                rs_copy(part_f, rs_f, rsf_s, rsf_r, m, c, peer(d), mp).wait_send()
-            for d in range(nmp):
-                ag_copy(own_f, rows, agf_s, agf_r, m, c, peer(d), mp, sec + 1).wait_send()
-
-    @pl.when(sec > 0)
-    def _():
-        @pl.loop(0, nb * CHUNKS)
-        def _(i):
-            m, c = i // CHUNKS, lax.rem(i, CHUNKS)
-            for d in range(1, nmp):
-                rs_copy(part_b, rs_b, rsb_s, rsb_r, m, c, peer(d), mp).wait_send()
-            for d in range(nmp):
-                ag_copy(own_b, grads, agb_s, agb_r, m, c, peer(d), mp, sec - 1).wait_send()
+    def settle(copy, active):
+        @pl.when(active)
+        def _():
+            @pl.loop(0, nb * CHUNKS)
+            def _(i):
+                for d in range(nmp):
+                    copy(i // CHUNKS, lax.rem(i, CHUNKS), peer(d)).wait_send()
+
+    settle(lambda m, c, j: rs_copy(part_f, rs_f, rsf_s, rsf_r, m, c, j, mp), sec < last)
+    settle(lambda m, c, j: rs_copy(part_b, rs_b, rsb_s, rsb_r, m, c, j, mp), sec > 0)
+    settle(lambda m, c, j: ag_copy(own_f, rows, agf_s, agf_r, m, c, j, mp, mate), mate < last)
+    settle(lambda m, c, j: ag_copy(own_b, grads, agb_s, agb_r, m, c, j, mp, mate), mate > 0)
 
 
 def local(ndp, nsec, nmp, hidden_in, slot_hidden, norm_gain, w_query, w_key, w_value, w_out,
@@ -498,6 +487,7 @@
             pltpu.VMEM((nb, padded, kw), BF16),
             pltpu.VMEM((nb, padded, kw), BF16),
             pltpu.VMEM((nb, groups, per * count, padded), F32),
+            pltpu.VMEM((nb, count, HD), F32),
             pltpu.VMEM((count, qw), BF16),
             pltpu.VMEM((count, qw), BF16),
             pltpu.VMEM((count, qw + 2 * kw), BF16),
@@ -515,8 +505,8 @@
         compiler_params=pltpu.CompilerParams(
             collective_id=0, has_side_effects=True, vmem_limit_bytes=58 * 1024 * 1024
         ),
-    )(hidden_in, slots, norm_gain, w_query, w_key, w_value, w_out, key_a, key_b, value_a, value_b,
-      cotangent)
+    )(hidden_in, slots, norm_gain, w_query, w_key, w_value, w_out, jnp.swapaxes(key_a, 1, 2), key_b,
+      jnp.swapaxes(value_a, 1, 2), value_b, cotangent)
     grad_a = jnp.einsum("psd,ptsr->tdr", sn_all.astype(F32), low_total, precision=HIGH)
     grad_b = jnp.einsum("ptsr,ptsc->trc", low_all, ks_all, preferred_element_type=F32)
     return (grad_a[None], grad_b[None])

time: 323 us -> 226 us (0.70)
  Pallas kernels: 313 us -> 221 us
  local copies, waits for them, and re-layouts: 4.72 us -> 0.01 us
    pallas_call x1, Pallas kernels: 313 us -> 221 us  [local(): pl.pallas_call(functools.partial(kernel, ndp, nsec, nmp), out_shape=(jax....]
    unnamed x6 -> x4, local copies, waits for them, and re-layouts: 4.72 us -> 0.01 us
where the time goes in v2:
time: 226 us
  Pallas kernels  221 us (98%)
  matrix products  4.32 us (2%)
    pallas_call x1, Pallas kernels, local(): pl.pallas_call(functools.partial(kernel, ndp, nsec, nmp), out_shape=(jax....  221 us

profile of v2, /device:TPU:0, one launch (start us, length us, event | category | flops | bytes accessed | tf_op | source)
XLA Modules:
  0.0 225.9 jit_solution(15533542995967226608)
XLA Ops:
  0.6 220.9 %shard_map.131 = (bf16[2,32,4096]{2,1,0:T(8,128)(2,1)}, bf16[2,2,32,64]{3,2,1,0:T(8,128)(2,1)}, f32[2,2,32,64]{3,2,1,0:T(8,128)}, bf16[2,2,32,256]{3,2,1,0:T(8,128)(2,1)}) custom-call(bf16[2,128,4096]{2,1,0:T(8,128)(2,1)} %hidden.1, bf16[1,32,4096]{2,1,0:T(8,128)(2,1)} %bitcast.22, f32[1,4096]{1,0:T(1,128)} %gain.1, bf16[1,4096,768]{2,1,0:T(8,128)(2,1)} %w_q.1, ...), custom_call_target="tpu_custom_call" | custom-call | tf_op jit(solution)/shard_map/pallas_call | solution.py:464
  221.6 0.0 copy-start
  221.6 0.0 copy-start.1
  221.6 3.5 %convolution_bitcast_fusion = f32[1,2,4096,64]{2,3,1,0:T(8,128)} fusion(f32[2,2,32,64]{3,2,1,0:T(8,128)} %get-tuple-element.6, bf16[2,32,4096]{2,1,0:T(8,128)(2,1)} %get-tuple-element.7), kind=kOutput, calls=%fused_computation | convolution fusion | flops 402653184 | bytes 2654208 | tf_op jit(solution)/shard_map/psd,ptsr->tdr/dot_general | solution.py:510
  225.0 0.0 copy-done
  225.0 0.0 copy-done.1
  225.0 0.9 convolution_bitcast_fusion.1
Async XLA Ops:
  221.6 3.5 %copy-start = (bf16[2,2,32,256]{3,2,1,0:T(8,128)(2,1)S(1)}, bf16[2,2,32,256]{3,2,1,0:T(8,128)(2,1)}, u32[]{:S(2)}) copy-start(bf16[2,2,32,256]{3,2,1,0:T(8,128)(2,1)} %get-tuple-element.9) | copy-start | bytes 196612
  221.6 3.5 %copy-start.1 = (bf16[2,2,32,64]{3,2,1,0:T(8,128)(2,1)S(1)}, bf16[2,2,32,64]{3,2,1,0:T(8,128)(2,1)}, u32[]{:S(2)}) copy-start(bf16[2,2,32,64]{3,2,1,0:T(8,128)(2,1)} %get-tuple-element.8) | copy-start | bytes 49156

commit v3 on v2

--- a/solution.py
+++ b/solution.py
@@ -13,7 +13,8 @@
 NEG = -1e30
 HIGH = lax.Precision.HIGHEST
 MESH = pl.DeviceIdType.MESH
-CHUNKS = 4
+CHUNKS = 8
+SPLIT = 2
 F32 = jnp.float32
 BF16 = jnp.bfloat16
 
@@ -203,6 +204,9 @@
     def cols(c):
         return pl.ds(pl.multiple_of(c * ch, ch), ch)
 
+    def wide_cols(c):
+        return pl.ds(pl.multiple_of(c * ch * SPLIT, ch * SPLIT), ch * SPLIT)
+
     def share_rows(j):
         return pl.ds(pl.multiple_of(j * share, share), share)
 
@@ -262,10 +266,7 @@
         parts = []
         for h in range(per):
             low = (g * per + h) * HD
-            if lead is None:
-                parts.append(ref[:, low : low + HD])
-            else:
-                parts.append(ref[lead, :, low : low + HD])
+            parts.append(ref[lead, :, low : low + HD])
         return jnp.concatenate(parts, axis=0)
 
     def forward(m):
@@ -281,13 +282,10 @@
             xn[at, :] = (x * inv * gain[...]).astype(BF16)
             inv_all[m, at, :] = jnp.broadcast_to(inv, (16, HD))
 
-        @pl.loop(0, per)
-        def _(i):
-            at = pl.ds(pl.multiple_of(i * kw, kw), kw)
-            q[m, :, at] = dot(xn[...], w_all[:, at]).astype(BF16)
-
-        kpad[m, 0:count, :] = dot(xn[...], w_all[:, qw : qw + kw]).astype(BF16)
-        vpad[m, 0:count, :] = dot(xn[...], w_all[:, qw + kw : qw + 2 * kw]).astype(BF16)
+        qkv = dot(xn[...], w_all[...]).astype(BF16)
+        q[m] = qkv[:, :qw]
+        kpad[m, 0:count, :] = qkv[:, qw : qw + kw]
+        vpad[m, 0:count, :] = qkv[:, qw + kw :]
         i_at = lax.rem(lax.broadcasted_iota(jnp.int32, (per * count, padded), 0), count)
         j_at = lax.broadcasted_iota(jnp.int32, (per * count, padded), 1)
         seen = (j_at <= i_at) | ((j_at >= count) & (j_at < count + ns))
@@ -305,27 +303,27 @@
 
         @pl.when(sec < last)
         def _():
-            @pl.loop(0, CHUNKS)
+            @pl.loop(0, CHUNKS // SPLIT)
             def _(c):
-                term = dot(mixed[...], w_o[:, cols(c)])
-                term = term + jnp.where(mine, rows[m, :, cols(c)].astype(F32), 0.0)
-                part_f[m, :, cols(c)] = term.astype(BF16)
-                rs_send(part_f, rs_f, rsf_s, rsf_r, m, c)
+                term = dot(mixed[...], w_o[:, wide_cols(c)])
+                term = term + jnp.where(mine, rows[m, :, wide_cols(c)].astype(F32), 0.0)
+                part_f[m, :, wide_cols(c)] = term.astype(BF16)
+                for k in range(SPLIT):
+                    rs_send(part_f, rs_f, rsf_s, rsf_r, m, c * SPLIT + k)
+
+    def mix_back(m):
+        gmix[m] = dot_nt(grads[m], w_o[...]).astype(BF16)
 
     def backward(m):
         @pl.when(sec < last)
         def _():
             ag_wait(own_b, grads, agb_s, agb_r, m, mate)
-
-        @pl.loop(0, per)
-        def _(i):
-            at = pl.ds(pl.multiple_of(i * kw, kw), kw)
-            gmix[:, at] = dot_nt(grads[m], w_o[at, :]).astype(BF16)
+            mix_back(m)
 
         at_slot = pl.ds(pl.multiple_of(m * ns, ns), ns)
         for g in range(groups):
             gc = slice(g * HD, (g + 1) * HD)
-            gm = stacked(gmix, None, g)
+            gm = stacked(gmix, m, g)
             p = probs[m, g]
             kg = kpad[m, :, gc]
             gp = dot_nt(gm, vpad[m, :, gc])
@@ -360,13 +358,20 @@
             )
             weight = weight * inv * (1.0 / width)
 
-            @pl.loop(0, CHUNKS)
+            @pl.loop(0, CHUNKS // SPLIT)
             def _(c):
-                term = dot_nt(dqkv[...], w_all[cols(c), :]) * gain[:, cols(c)]
-                term = inv * (term - rows[m, :, cols(c)].astype(F32) * weight)
-                term = term + jnp.where(mine, grads[m, :, cols(c)].astype(F32), 0.0)
-                part_b[m, :, cols(c)] = term.astype(BF16)
-                rs_send(part_b, rs_b, rsb_s, rsb_r, m, c)
+                term = dot_nt(dqkv[...], w_all[wide_cols(c), :]) * gain[:, wide_cols(c)]
+                term = inv * (term - rows[m, :, wide_cols(c)].astype(F32) * weight)
+                term = term + jnp.where(mine, grads[m, :, wide_cols(c)].astype(F32), 0.0)
+                part_b[m, :, wide_cols(c)] = term.astype(BF16)
+                for k in range(SPLIT):
+                    rs_send(part_b, rs_b, rsb_s, rsb_r, m, c * SPLIT + k)
+
+    @pl.when(sec == last)
+    def _():
+        @pl.loop(0, nb)
+        def _(m):
+            mix_back(m)
 
     low_half = sec < half
     f_at = jnp.where(low_half, 0, nb)
@@ -489,7 +494,7 @@
             pltpu.VMEM((nb, groups, per * count, padded), F32),
             pltpu.VMEM((nb, count, HD), F32),
             pltpu.VMEM((count, qw), BF16),
-            pltpu.VMEM((count, qw), BF16),
+            pltpu.VMEM((nb, count, qw), BF16),
             pltpu.VMEM((count, qw + 2 * kw), BF16),
             pltpu.VMEM(sn_shape, BF16),
             pltpu.VMEM(low_shape, BF16),

time: 226 us -> 225 us (level)
  no operation moved by 1% of the time
where the time goes in v3:
time: 225 us
  Pallas kernels  220 us (98%)
  matrix products  4.32 us (2%)
    pallas_call x1, Pallas kernels, local(): pl.pallas_call(functools.partial(kernel, ndp, nsec, nmp), out_shape=(jax....  220 us

profile of v3, /device:TPU:0, one launch (start us, length us, event | category | flops | bytes accessed | tf_op | source)
XLA Modules:
  0.0 225.2 jit_solution(11784787568637314107)
XLA Ops:
  0.6 220.2 %shard_map.131 = (bf16[2,32,4096]{2,1,0:T(8,128)(2,1)}, bf16[2,2,32,64]{3,2,1,0:T(8,128)(2,1)}, f32[2,2,32,64]{3,2,1,0:T(8,128)}, bf16[2,2,32,256]{3,2,1,0:T(8,128)(2,1)}) custom-call(bf16[2,128,4096]{2,1,0:T(8,128)(2,1)} %hidden.1, bf16[1,32,4096]{2,1,0:T(8,128)(2,1)} %bitcast.22, f32[1,4096]{1,0:T(1,128)} %gain.1, bf16[1,4096,768]{2,1,0:T(8,128)(2,1)} %w_q.1, ...), custom_call_target="tpu_custom_call" | custom-call | tf_op jit(solution)/shard_map/pallas_call | solution.py:469
  220.9 0.0 copy-start
  220.9 0.0 copy-start.1
  220.9 3.5 %convolution_bitcast_fusion = f32[1,2,4096,64]{2,3,1,0:T(8,128)} fusion(f32[2,2,32,64]{3,2,1,0:T(8,128)} %get-tuple-element.6, bf16[2,32,4096]{2,1,0:T(8,128)(2,1)} %get-tuple-element.7), kind=kOutput, calls=%fused_computation | convolution fusion | flops 402653184 | bytes 2654208 | tf_op jit(solution)/shard_map/psd,ptsr->tdr/dot_general | solution.py:515
  224.3 0.0 copy-done
  224.3 0.0 copy-done.1
  224.3 0.9 convolution_bitcast_fusion.1
Async XLA Ops:
  220.9 3.5 %copy-start = (bf16[2,2,32,256]{3,2,1,0:T(8,128)(2,1)S(1)}, bf16[2,2,32,256]{3,2,1,0:T(8,128)(2,1)}, u32[]{:S(2)}) copy-start(bf16[2,2,32,256]{3,2,1,0:T(8,128)(2,1)} %get-tuple-element.9) | copy-start | bytes 196612
  220.9 3.5 %copy-start.1 = (bf16[2,2,32,64]{3,2,1,0:T(8,128)(2,1)S(1)}, bf16[2,2,32,64]{3,2,1,0:T(8,128)(2,1)}, u32[]{:S(2)}) copy-start(bf16[2,2,32,64]{3,2,1,0:T(8,128)(2,1)} %get-tuple-element.8) | copy-start | bytes 49156

commit v4 on v3

--- a/solution.py
+++ b/solution.py
@@ -98,7 +98,10 @@
     mp = lax.axis_index("mp")
     last = nsec - 1
     half = nsec // 2
-    mate = lax.rem(sec + half, nsec)
+    f_from = lax.rem(sec + 1, last)
+    f_owner = lax.rem(sec + last - 1, last)
+    b_from = last - lax.rem(last - sec + 1, last)
+    b_owner = last - lax.rem(last - sec + last - 1, last)
     nb, count, width = rows.shape
     ns = slots.shape[1] // nb
     share = count // nmp
@@ -219,7 +222,7 @@
             dst_ref=land.at[m, source, :, cols(c)],
             send_sem=send.at[sem_at(m, c, to)],
             recv_sem=recv.at[sem_at(m, c, source)],
-            device_id={"section": mate, "mp": to},
+            device_id={"section": f_owner if part is part_f else b_owner, "mp": to},
             device_id_type=MESH,
         )
 
@@ -272,7 +275,7 @@
     def forward(m):
         @pl.when(sec > 0)
         def _():
-            ag_wait(own_f, rows, agf_s, agf_r, m, mate)
+            ag_wait(own_f, rows, agf_s, agf_r, m, lax.rem(sec + 1, nsec))
 
         @pl.loop(0, count // 16)
         def _(i):
@@ -317,7 +320,7 @@
     def backward(m):
         @pl.when(sec < last)
         def _():
-            ag_wait(own_b, grads, agb_s, agb_r, m, mate)
+            ag_wait(own_b, grads, agb_s, agb_r, m, lax.rem(sec + 1, nsec))
             mix_back(m)
 
         at_slot = pl.ds(pl.multiple_of(m * ns, ns), ns)
@@ -381,9 +384,9 @@
 
     @pl.loop(0, 4 * nb)
     def _(t):
-        @pl.when((mate < last) & (t >= rf_at) & (t < rf_at + nb))
-        def _():
-            reduce(own_f, part_f, rs_f, rows, rsf_s, rsf_r, agf_s, agf_r, t - rf_at, mate + 1)
+        @pl.when((sec < last) & (t >= rf_at) & (t < rf_at + nb))
+        def _():
+            reduce(own_f, part_f, rs_f, rows, rsf_s, rsf_r, agf_s, agf_r, t - rf_at, f_from + 1)
 
         @pl.when((t >= f_at) & (t < f_at + nb))
         def _():
@@ -393,9 +396,9 @@
         def _():
             backward(t - b_at)
 
-        @pl.when((mate > 0) & (t >= rb_at) & (t < rb_at + nb))
-        def _():
-            reduce(own_b, part_b, rs_b, grads, rsb_s, rsb_r, agb_s, agb_r, t - rb_at, mate - 1)
+        @pl.when((sec > 0) & (t >= rb_at) & (t < rb_at + nb))
+        def _():
+            reduce(own_b, part_b, rs_b, grads, rsb_s, rsb_r, agb_s, agb_r, t - rb_at, b_from - 1)
 
     dp_send(ks_all, ks_s, ks_r)
     me = dp * nmp + mp
@@ -442,8 +445,8 @@
 
     settle(lambda m, c, j: rs_copy(part_f, rs_f, rsf_s, rsf_r, m, c, j, mp), sec < last)
     settle(lambda m, c, j: rs_copy(part_b, rs_b, rsb_s, rsb_r, m, c, j, mp), sec > 0)
-    settle(lambda m, c, j: ag_copy(own_f, rows, agf_s, agf_r, m, c, j, mp, mate), mate < last)
-    settle(lambda m, c, j: ag_copy(own_b, grads, agb_s, agb_r, m, c, j, mp, mate), mate > 0)
+    settle(lambda m, c, j: ag_copy(own_f, rows, agf_s, agf_r, m, c, j, mp, f_from + 1), sec < last)
+    settle(lambda m, c, j: ag_copy(own_b, grads, agb_s, agb_r, m, c, j, mp, b_from - 1), sec > 0)
 
 
 def local(ndp, nsec, nmp, hidden_in, slot_hidden, norm_gain, w_query, w_key, w_value, w_out,

time: 225 us -> 238 us (1.058)
  Pallas kernels: 220 us -> 233 us
    pallas_call x1, Pallas kernels: 220 us -> 233 us  [local(): pl.pallas_call(functools.partial(kernel, ndp, nsec, nmp), out_shape=(jax....]
where the time goes in v4:
time: 238 us
  Pallas kernels  233 us (98%)
  matrix products  4.32 us (2%)
    pallas_call x1, Pallas kernels, local(): pl.pallas_call(functools.partial(kernel, ndp, nsec, nmp), out_shape=(jax....  233 us

profile of v4, /device:TPU:0, one launch (start us, length us, event | category | flops | bytes accessed | tf_op | source)
XLA Modules:
  0.0 238.0 jit_solution(16906091517960937195)
XLA Ops:
  0.6 233.1 %shard_map.131 = (bf16[2,32,4096]{2,1,0:T(8,128)(2,1)}, bf16[2,2,32,64]{3,2,1,0:T(8,128)(2,1)}, f32[2,2,32,64]{3,2,1,0:T(8,128)}, bf16[2,2,32,256]{3,2,1,0:T(8,128)(2,1)}) custom-call(bf16[2,128,4096]{2,1,0:T(8,128)(2,1)} %hidden.1, bf16[1,32,4096]{2,1,0:T(8,128)(2,1)} %bitcast.22, f32[1,4096]{1,0:T(1,128)} %gain.1, bf16[1,4096,768]{2,1,0:T(8,128)(2,1)} %w_q.1, ...), custom_call_target="tpu_custom_call" | custom-call | tf_op jit(solution)/shard_map/pallas_call | solution.py:472
  233.7 0.0 copy-start
  233.7 0.0 copy-start.1
  233.7 3.5 %convolution_bitcast_fusion = f32[1,2,4096,64]{2,3,1,0:T(8,128)} fusion(f32[2,2,32,64]{3,2,1,0:T(8,128)} %get-tuple-element.6, bf16[2,32,4096]{2,1,0:T(8,128)(2,1)} %get-tuple-element.7), kind=kOutput, calls=%fused_computation | convolution fusion | flops 402653184 | bytes 2654208 | tf_op jit(solution)/shard_map/psd,ptsr->tdr/dot_general | solution.py:518
  237.2 0.0 copy-done
  237.2 0.0 copy-done.1
  237.2 0.9 convolution_bitcast_fusion.1
Async XLA Ops:
  233.7 3.5 %copy-start = (bf16[2,2,32,256]{3,2,1,0:T(8,128)(2,1)S(1)}, bf16[2,2,32,256]{3,2,1,0:T(8,128)(2,1)}, u32[]{:S(2)}) copy-start(bf16[2,2,32,256]{3,2,1,0:T(8,128)(2,1)} %get-tuple-element.9) | copy-start | bytes 196612
  233.7 3.5 %copy-start.1 = (bf16[2,2,32,64]{3,2,1,0:T(8,128)(2,1)S(1)}, bf16[2,2,32,64]{3,2,1,0:T(8,128)(2,1)}, u32[]{:S(2)}) copy-start(bf16[2,2,32,64]{3,2,1,0:T(8,128)(2,1)} %get-tuple-element.8) | copy-start | bytes 49156
